TPU v7x, 256 devices: a whole 4x4x8 slice. The times are simulated.
256 devices in a mesh: row: 16 (over y, z_lo), col: 16 (over x, z_hi, core).
Axes of the slice: x: 4, y: 4, z: 8 (z_hi: 2, z_lo: 4; z = z_hi * 4 + z_lo), core: 2. Of those that a mesh axis runs over, the one named last changes fastest.
Arguments:
- matrix: bfloat16 [8192, 8192], P('row', 'col'), may hold values from 0 to 0.0024414062, as said below
- in_mask: int32 [32, 32], P('row', 'col'), may hold values from 0 to 1, as said below
- out_mask: int32 [32, 32], P('row', 'col'), may hold values from 0 to 1, as said below
Outputs:
- flow: float32 [8192, 8192], P('row', 'col')
Inputs may be any that keep to these rules, and one draw needn't show every extreme that they name: `matrix`: every diagonal entry is positive; all other entries are zero or positive. `in_mask`: tiles on the diagonal are 1. The block of tiles of one device holds at most 3 ones, and some device's block holds exactly 3. `out_mask`: tiles on the diagonal are 1.
All inputs are finite; a program needn't handle non-finite values.
Results may differ from a plain program's by a relative error of at most 0.0003.
Values may be sent and summed in bfloat16 or wider, within the bound.
A program may use at most 128 MiB of HBM per device.

v0:
```python
import jax
import jax.numpy as jnp
from jax import lax
from jax.sharding import PartitionSpec as P


def expand_mask(values, tile_flags):
    tile_rows, tile_cols = tile_flags.shape
    shaped = values.reshape(
        tile_rows, values.shape[0] // tile_rows, tile_cols, values.shape[1] // tile_cols
    )
    return (shaped * tile_flags.astype(values.dtype)[:, None, :, None]).reshape(values.shape)


def masked_product(left_part, left_flags, right_part, right_flags):
    return jnp.dot(
        expand_mask(left_part, left_flags),
        expand_mask(right_part, right_flags),
        preferred_element_type=jnp.float32,
    )


def per_device(matrix, in_mask, out_mask):
    local_rows, local_cols = matrix.shape
    col_values, col_flags = (
        lax.all_gather(matrix, "row", axis=0, tiled=True),
        lax.all_gather(in_mask, "row", axis=0, tiled=True),
    )
    piece_values = lax.all_gather(matrix, "col", axis=1, tiled=True)
    piece_flags = lax.all_gather(in_mask, "col", axis=1, tiled=True)
    product = masked_product(piece_values, piece_flags, col_values, col_flags)
    inflated = expand_mask(product * product, out_mask)
    partial_sums = jnp.sum(inflated, axis=0)
    totals = lax.psum(partial_sums, "row")
    total_rows = float(local_rows * lax.axis_size("row"))
    return total_rows * inflated / totals[None, :]


def solution(mesh):
    placed = (P("row", "col"), P("row", "col"), P("row", "col"))
    return jax.shard_map(
        per_device, mesh=mesh, in_specs=placed, out_specs=P("row", "col"), check_vma=False
    )
```

profile of v0, /device:TPU:2, one launch (start us, length us, event | category | flops | bytes accessed | tf_op | source)
XLA Modules:
  0.0 372.1 jit_solution(11102668972356177481)
XLA Ops:
  6.5 0.0 all-gather.5.cloned.1.call-start
  6.5 0.7 all-gather.5.cloned.1.call-update
  7.3 0.0 all-gather.7.cloned.1.call-start
  7.3 0.7 all-gather.7.cloned.1.call-update
  8.0 0.8 copy.16
  8.8 35.7 %all-gather = s32[16,2,2]{2,1,0:T(2,128)S(1)} all-gather(s32[1,2,2]{2,1,0:T(2,128)S(1)} %bitcast.25), channel_id=1, replica_groups=mesh['row'=16,'col'=16] {'col'}, dimensions={0}, use_global_device_ids=true | all-gather | bytes 272 | tf_op jit(solution)/shard_map/all_gather | solution.py:30
  44.5 0.1 copy.17
  44.5 0.1 copy.18
  44.7 0.1 reshape.18
  44.8 4.3 %mul.42 = bf16[2,256,32,256]{3,2,1,0:T(8,128)(2,1)} broadcast(bf16[2,32]{1,0:T(2,128)(2,1)S(1)} %bitcast.26), dimensions={0,2} | broadcast | bytes 8388736 | tf_op jit(solution)/shard_map/mul | solution.py:12
  49.1 0.0 copy-start
  49.1 16.4 %copy.24 = bf16[64,8,32,256]{3,1,2,0:T(8,128)(2,1)} copy(bf16[64,8,32,256]{3,2,1,0:T(8,128)(2,1)} %bitcast.16) | data formatting | bytes 16777216
  65.6 0.0 copy-done
  65.6 42.5 %all-gather.1 = s32[16,2,2]{2,1,0:T(2,128)S(1)} all-gather(s32[1,2,2]{2,1,0:T(2,128)S(1)} %bitcast.24), channel_id=1, replica_groups=mesh['row'=16,'col'=16] {'row'}, dimensions={0}, use_global_device_ids=true | all-gather | bytes 272 | tf_op jit(solution)/shard_map/all_gather | solution.py:27
  108.1 0.1 copy.19
  108.2 0.1 copy.22
  108.3 6.6 %mul.45 = bf16[32,256,2,256]{3,2,1,0:T(2,128)(2,1)} broadcast(bf16[32,2]{1,0:T(8,128)(2,1)S(1)} %bitcast.22), dimensions={0,2} | broadcast | bytes 8388736 | tf_op jit(solution)/shard_map/mul | solution.py:12
  114.9 0.0 copy-start.1
  114.9 8.6 %copy.25 = bf16[1024,8,2,256]{3,1,2,0:T(8,128)(2,1)} copy(bf16[1024,8,2,256]{3,2,1,0:T(2,128)(2,1)} %bitcast.17) | data formatting | bytes 16777216
  123.6 0.0 copy-done.1
  123.6 0.3 mul.49
  123.9 0.1 copy.26
  124.0 2.5 all-gather.5.cloned.1.call-done
  126.5 185.0 %all-gather.7.cloned.1.call-done = bf16[8192,512]{1,0:T(8,128)(2,1)} async-done(((bf16[512,512]{1,0:T(8,128)(2,1)}), bf16[8192,512]{1,0:T(8,128)(2,1)}) %all-gather.7.cloned.1.call-update) | async-done | bytes 8388624 | tf_op jit(solution)/shard_map/all_gather | solution.py:26
  311.5 13.2 %fusion.13 = (f32[512]{0:T(512)S(1)}, f32[512,512]{1,0:T(8,128)S(1)}) fusion(f32[512,512]{1,0:T(8,128)S(1)} %bitcast.21, bf16[8192,512]{1,0:T(8,128)(2,1)} %all-gather.7.cloned.1.call-done, bf16[8192,512]{1,0:T(8,128)(2,1)} %bitcast.19, bf16[512,8192]{1,0:T(8,128)(2,1)} %all-gather.5.cloned.1.call-done, bf16[512,8192]{1,0:T(8,128)(2,1)} %bitcast.18), kind=kOutput, calls=%fused_computation.6 | convolution fusion | flops 4304141824 | bytes 35653632 | tf_op jit(solution)/shard_map/dot_general | solution.py:16
  324.8 39.3 %psum.7 = f32[512]{0:T(512)S(1)} all-reduce(f32[512]{0:T(512)S(1)} %get-tuple-element.5), channel_id=1, replica_groups=mesh['row'=16,'col'=16] {'row'}, use_global_device_ids=true, to_apply=%region_1.0 | all-reduce | flops 512 | bytes 4096 | tf_op jit(solution)/shard_map/psum | solution.py:34
  364.1 1.1 multiply_divide_fusion
  (3 shorter events, 0.0 us)
Async XLA Ops:
  6.5 120.0 %all-gather.5.cloned.1.call-start = ((), (), s32[]{:S(2)}) async-start(), calls=%async_computation | async-start | bytes 8912896 | tf_op jit(solution)/shard_map/all_gather | solution.py:29
  7.3 304.3 %all-gather.7.cloned.1.call-start = ((), (), s32[]{:S(2)}) async-start(), calls=%async_computation.1 | async-start | bytes 8912896 | tf_op jit(solution)/shard_map/all_gather | solution.py:26
  49.1 16.5 %copy-start = (s32[2,2]{1,0:T(2,128)S(1)}, s32[2,2]{1,0:T(2,128)}, u32[]{:S(2)}) copy-start(s32[2,2]{1,0:T(2,128)} %param.4) | copy-start | bytes 52
  114.9 8.7 %copy-start.1 = (s32[2,2]{1,0:T(2,128)S(1)}, s32[2,2]{1,0:T(2,128)}, u32[]{:S(2)}) copy-start(s32[2,2]{1,0:T(2,128)} %param.5) | copy-start | bytes 52
Sparse Core Ops, SparseCore 0:
  9.9 116.5 all-gather.4
  128.3 183.1 all-gather.6
where the time goes:
time: 372 us
  waiting for transfers between devices  189 us (51%)
  blocking collectives  118 us (32%)
  local copies, waits for them, and re-layouts  37.7 us (10%)
  between operations  13.4 us (4%)
  matrix products  13.2 us (4%)
    all_gather x1, waiting for transfers between devices, per_device(): lax.all_gather(matrix, 'row', axis=0, tiled=True)  185 us
    all_gather x1, blocking collectives, per_device(): lax.all_gather(in_mask, 'row', axis=0, tiled=True)  42.5 us
    psum x1, blocking collectives, per_device(): totals = lax.psum(partial_sums, 'row')  39.3 us
    all_gather x1, blocking collectives, per_device(): piece_flags = lax.all_gather(in_mask, 'col', axis=1, tiled=True)  35.7 us
    unnamed x8, local copies, waits for them, and re-layouts  25.9 us
    dot_general x1, matrix products, masked_product(): jnp.dot(expand_mask(left_part, left_flags), expand_mask(right_part, right...  13.2 us
    mul x3, local copies, waits for them, and re-layouts, expand_mask(): shaped * tile_flags.astype(values.dtype)[:, None, :, None]  11.3 us
  transfers between devices with their start and end apart: 2, of which 2 were waited for; matrix products, arithmetic and copies ran while one was open for 10% of the time, Pallas kernels for 0%

commit v1 on v0

v1 whole, which is shorter than its diff:
```python
import functools

import jax
import jax.numpy as jnp
from jax import lax
from jax.experimental import pallas as pl
from jax.experimental.pallas import tpu as pltpu
from jax.sharding import PartitionSpec as P

MESH = pl.DeviceIdType.MESH
T = 256
N = 2 * T
BODY = 3 * T
ROWS = BODY + 16
CUT = 400
HALF = ((0, CUT), (CUT, ROWS - CUT))
PAIRS = tuple((t, s) for t in range(4) for s in range(3) if s <= t)


def kernel(
    total_rows, m_ref, in_ref, om_ref, infl_ref, scale_ref,
    abuf, bbuf, ad, bd, acc, tot, part,
    ys, yr, zs, zr, xs, xr, cs, cr, ss, sr, ts, tr, osem,
):
    row = lax.axis_index("row")
    col = lax.axis_index("col")
    y, z = row // 4, row % 4
    x, h, core = col // 4, (col // 2) % 2, col % 2
    hi = z // 2
    yup, ydn = (y + 1) % 4, (y + 3) % 4
    xup, xdn = (x + 1) % 4, (x + 3) % 4
    zorder = (z, 1 - z + 4 * hi, 2 - hi, 3 - 3 * hi)
    horder = (h, 1 - h)

    def col_of(xx, hh, kk):
        return xx * 4 + hh * 2 + kk

    barrier = pltpu.get_barrier_semaphore()

    def greet(d, _):
        pl.semaphore_signal(barrier, inc=1, device_id=((row + d) % 16, col), device_id_type=MESH)
        return 0

    lax.fori_loop(1, 16, greet, 0)
    for c in (col_of(xup, h, core), col_of(xdn, h, core), col_of(x, 1 - h, core), col_of(x, h, 1 - core)):
        pl.semaphore_signal(barrier, inc=1, device_id=(row, c), device_id_type=MESH)

    flags = [in_ref[0, 0], in_ref[0, 1], in_ref[1, 0], in_ref[1, 1]]
    ranks = [0, flags[0], flags[0] + flags[1], flags[0] + flags[1] + flags[2]]
    here = {(t, s): jnp.logical_and(flags[t] == 1, ranks[t] == s) for t, s in PAIRS}
    mine_b = row
    mine_a = col
    for s in range(3):
        for r in range(0, T, 64):
            value = jnp.zeros((64, T), jnp.bfloat16)
            for t in range(s, 4):
                i, j = t // 2, t % 2
                tile = m_ref[i * T + r : i * T + r + 64, j * T : (j + 1) * T]
                value = lax.select(here[t, s], tile, value)
            bbuf[mine_b, pl.ds(s * T + r, 64), :] = value
            abuf[mine_a, pl.ds(s * T + r, 64), :] = value
    line = lax.broadcasted_iota(jnp.int32, (16, T), 0)
    weights = jnp.zeros((16, T), jnp.float32)
    for q, (t, s) in enumerate(PAIRS):
        weights = jnp.where(line == q, here[t, s].astype(jnp.float32), weights)
    weights = weights.astype(jnp.bfloat16)
    bbuf[mine_b, pl.ds(BODY, 16), :] = weights
    abuf[mine_a, pl.ds(BODY, 16), :] = weights

    pl.semaphore_wait(barrier, 19)

    def whole(buf, k, send, recv, device):
        return pltpu.make_async_remote_copy(
            src_ref=buf.at[k], dst_ref=buf.at[k], send_sem=send, recv_sem=recv,
            device_id=device, device_id_type=MESH,
        )

    def half(buf, k, p, send, recv, device):
        at = buf.at[k, pl.ds(*HALF[p]), :]
        return pltpu.make_async_remote_copy(
            src_ref=at, dst_ref=at, send_sem=send, recv_sem=recv,
            device_id=device, device_id_type=MESH,
        )

    def y_copy(i, way, piece):
        to = ((yup, ydn)[way] * 4 + z, col)
        if piece < 2:
            which, origin = (way, 1 - way)[piece], y
        else:
            which, origin = way, (ydn, yup)[way]
        return half(bbuf, origin * 4 + zorder[i], which, ys.at[i, way, piece], yr.at[i, way, piece], to)

    def y_arrival(i, way, piece):
        if piece < 2:
            which, origin = (way, 1 - way)[piece], (ydn, yup)[way]
        else:
            which, origin = way, (y + 2) % 4
        return half(bbuf, origin * 4 + zorder[i], which, ys.at[i, way, piece], yr.at[i, way, piece], ((yup, ydn)[way] * 4 + z, col))

    def x_copy(i, way, piece):
        to = (row, col_of((xup, xdn)[way], h, core))
        if piece < 2:
            which, origin = (way, 1 - way)[piece], x
        else:
            which, origin = way, (xdn, xup)[way]
        return half(abuf, col_of(origin, horder[i], core), which, xs.at[i, way, piece], xr.at[i, way, piece], to)

    def x_arrival(i, way, piece):
        if piece < 2:
            which, origin = (way, 1 - way)[piece], (xdn, xup)[way]
        else:
            which, origin = way, (x + 2) % 4
        return half(abuf, col_of(origin, horder[i], core), which, xs.at[i, way, piece], xr.at[i, way, piece], (row, col_of((xup, xdn)[way], h, core)))

    def s_copy(i, d):
        k = col_of((x + d) % 4, horder[i], core)
        return whole(abuf, k, ss.at[i, d], sr.at[i, d], (row, col_of(x, h, 1 - core)))

    def s_arrival(i, d):
        k = col_of((x + d) % 4, horder[i], 1 - core)
        return whole(abuf, k, ss.at[i, d], sr.at[i, d], (row, col_of(x, h, 1 - core)))

    cross = whole(abuf, mine_a, cs, cr, (row, col_of(x, 1 - h, core)))
    crossed = whole(abuf, col_of(x, 1 - h, core), cs, cr, (row, col_of(x, 1 - h, core)))

    z_up = whole(bbuf, row, zs.at[0], zr.at[z], (row + 1, col))
    z_down = whole(bbuf, row, zs.at[1], zr.at[z], (row - 1, col))
    has_up, has_down = z < 3, z > 0
    interior = jnp.logical_and(has_up, has_down)
    at_end = jnp.logical_not(interior)

    def z_forward(i):
        to = y * 4 + (3 - z if i == 1 else 3 * hi)
        k = y * 4 + zorder[i]
        return whole(bbuf, k, zs.at[1 + i], zr.at[zorder[i]], (to, col))

    def z_arrival(i):
        k = y * 4 + zorder[i]
        return whole(bbuf, k, zs.at[1 + i], zr.at[zorder[i]], (y * 4 + (z + 1) % 4, col))

    def y_send(i):
        for piece in range(2):
            for way in range(2):
                y_copy(i, way, piece).start()

    def y_turn(i):
        for way in range(2):
            y_arrival(i, way, 0).wait_recv()
            y_copy(i, way, 2).start()

    def x_send(i):
        for piece in range(2):
            for way in range(2):
                x_copy(i, way, piece).start()

    def x_turn(i):
        for way in range(2):
            x_arrival(i, way, 0).wait_recv()
            x_copy(i, way, 2).start()

    def z_turn(i):
        z_arrival(i).wait_recv()
        pl.when(interior)(lambda: z_forward(i).start())

    def x_near(i):
        for way in range(2):
            x_arrival(i, way, 1).wait_recv()
            s_copy(i, (3, 1)[way]).start()

    def x_far(i):
        for way in range(2):
            x_arrival(i, way, 2).wait_recv()
        s_copy(i, 2).start()

    def expand(buf, k, to):
        ext = buf[k, pl.ds(BODY, 16), :].astype(jnp.float32)
        w = {
            ts_: jnp.broadcast_to(ext[q : q + 1, :], (16, T)).astype(jnp.bfloat16)[None]
            for q, ts_ in enumerate(PAIRS)
        }
        for t in range(4):
            i, j = t // 2, t % 2
            value = None
            for s in range(min(t, 2) + 1):
                term = buf[k, pl.ds(s * T, T), :].reshape(16, 16, T) * w[t, s]
                value = term if value is None else value + term
            to[i * T : (i + 1) * T, j * T : (j + 1) * T] = value.reshape(T, T)

    def product(k):
        expand(abuf, k, ad)
        expand(bbuf, k, bd)
        acc[...] += jnp.dot(ad[...], bd[...], preferred_element_type=jnp.float32)

    def products(i, offsets):
        first, count = offsets
        lax.fori_loop(first, first + count, lambda d, _: (product(((y + d) % 4) * 4 + zorder[i]), 0)[1], 0)

    @pl.when(has_up)
    def _():
        z_up.start()

    @pl.when(has_down)
    def _():
        z_down.start()

    y_send(0)
    x_send(0)
    s_copy(0, 0).start()
    acc[...] = jnp.zeros_like(acc)
    y_turn(0)
    x_turn(0)
    z_turn(1)
    pl.when(interior)(lambda: z_turn(2))
    cross.start()
    y_send(1)
    x_near(0)
    x_far(0)
    y_turn(1)
    pl.when(interior)(lambda: z_turn(3))
    pl.when(at_end)(lambda: z_arrival(2).wait_recv())
    y_send(2)
    crossed.wait_recv()
    x_send(1)
    s_copy(1, 0).start()
    y_turn(2)
    pl.when(at_end)(lambda: z_arrival(3).wait_recv())
    y_send(3)
    x_turn(1)
    x_near(1)
    x_far(1)
    for i in range(2):
        for d in range(4):
            s_arrival(i, d).wait_recv()

    def y_rest(i):
        for way in range(2):
            y_arrival(i, way, 1).wait_recv()
            y_arrival(i, way, 2).wait_recv()

    y_rest(0)
    products(0, (0, 4))
    y_turn(3)
    y_rest(1)
    products(1, (0, 4))
    y_rest(2)
    products(2, (0, 4))
    products(3, (0, 1))
    for way in range(2):
        y_arrival(3, way, 1).wait_recv()
    products(3, (1, 1))
    products(3, (3, 1))
    for way in range(2):
        y_arrival(3, way, 2).wait_recv()
    products(3, (2, 1))

    sums = jnp.zeros((8, N), jnp.float32)
    pieces = [[None, None], [None, None]]
    for i in range(2):
        keep = [(om_ref[i, j] == 1).astype(jnp.float32) for j in range(2)]
        for r in range(i * T, (i + 1) * T, 32):
            for j in range(2):
                at = (slice(r, r + 32), slice(j * T, (j + 1) * T))
                p = acc[at]
                v = p * p * keep[j]
                acc[at] = v
                v = v.reshape(4, 8, T).sum(axis=0)
                pieces[i][j] = v if pieces[i][j] is None else pieces[i][j] + v
    sums = jnp.concatenate([pieces[0][j] + pieces[1][j] for j in range(2)], axis=1)
    sums = jnp.sum(sums, axis=0, keepdims=True)
    part[...] = sums
    tot[row] = sums

    def t_copy(d):
        return pltpu.make_async_remote_copy(
            src_ref=part, dst_ref=tot.at[row], send_sem=ts.at[d], recv_sem=tr.at[d],
            device_id=((row + d) % 16, col), device_id_type=MESH,
        )

    def t_arrival(d):
        return pltpu.make_async_remote_copy(
            src_ref=part, dst_ref=tot.at[(row + 16 - d) % 16], send_sem=ts.at[d], recv_sem=tr.at[d],
            device_id=((row + d) % 16, col), device_id_type=MESH,
        )

    lax.fori_loop(1, 16, lambda d, _: (t_copy(d).start(), 0)[1], 0)
    out = pltpu.make_async_copy(acc, infl_ref, osem)
    out.start()
    lax.fori_loop(1, 16, lambda d, _: (t_arrival(d).wait_recv(), 0)[1], 0)
    total = tot[0]
    for d in range(1, 16):
        total = total + tot[d]
    scale_ref[...] = 1.0 / total
    out.wait()

    lax.fori_loop(1, 16, lambda d, _: (t_copy(d).wait_send(), 0)[1], 0)
    for i in range(4):
        for way in range(2):
            for piece in range(3):
                y_copy(i, way, piece).wait_send()
    for i in range(2):
        for way in range(2):
            for piece in range(3):
                x_copy(i, way, piece).wait_send()
        for d in range(4):
            s_copy(i, d).wait_send()
    cross.wait_send()

    @pl.when(has_up)
    def _():
        z_up.wait_send()

    @pl.when(has_down)
    def _():
        z_down.wait_send()

    @pl.when(interior)
    def _():
        for i in range(1, 4):
            z_forward(i).wait_send()


def solution(mesh):
    def step(matrix, in_mask, out_mask):
        total_rows = float(N * mesh.shape["row"])
        dma = pltpu.SemaphoreType.DMA
        inflated, scale = pl.pallas_call(
            functools.partial(kernel, total_rows),
            out_shape=(
                jax.ShapeDtypeStruct((N, N), jnp.float32),
                jax.ShapeDtypeStruct((1, N), jnp.float32),
            ),
            in_specs=[
                pl.BlockSpec(memory_space=pltpu.VMEM),
                pl.BlockSpec(memory_space=pltpu.SMEM),
                pl.BlockSpec(memory_space=pltpu.SMEM),
            ],
            out_specs=(
                pl.BlockSpec(memory_space=pl.ANY),
                pl.BlockSpec(memory_space=pltpu.VMEM),
            ),
            scratch_shapes=[
                pltpu.VMEM((16, ROWS, T), jnp.bfloat16),
                pltpu.VMEM((16, ROWS, T), jnp.bfloat16),
                pltpu.VMEM((N, N), jnp.bfloat16),
                pltpu.VMEM((N, N), jnp.bfloat16),
                pltpu.VMEM((N, N), jnp.float32),
                pltpu.VMEM((16, 1, N), jnp.float32),
                pltpu.VMEM((1, N), jnp.float32),
                dma((4, 2, 3)), dma((4, 2, 3)),
                dma((5,)), dma((4,)),
                dma((2, 2, 3)), dma((2, 2, 3)),
                dma, dma,
                dma((2, 4)), dma((2, 4)),
                dma((16,)), dma((16,)),
                dma,
            ],
            compiler_params=pltpu.CompilerParams(
                collective_id=0, has_side_effects=True, vmem_limit_bytes=40 * 1024 * 1024
            ),
            name="gather_square",
        )(matrix, in_mask, out_mask)
        return (total_rows * inflated) * scale

    placed = (P("row", "col"), P("row", "col"), P("row", "col"))
    return jax.shard_map(
        step, mesh=mesh, in_specs=placed, out_specs=P("row", "col"), check_vma=False
    )
```

time: 372 us -> 83.5 us (0.22)
  the two profiles are of different devices: /device:TPU:2 before, /device:TPU:1 now
where the time goes in v1:
time: 83.5 us; the launch traced here: 83.3 us
  Pallas kernels  79.8 us (96%)
  local copies, waits for them, and re-layouts  2.4 us (3%)
  other arithmetic  1.1 us (1%)
    pallas_call x1, Pallas kernels, step(): pl.pallas_call(functools.partial(kernel, total_rows), out_shape=(jax.Shap...  79.8 us
    unnamed x6, local copies, waits for them, and re-layouts  2.4 us

profile of v1, /device:TPU:1, one launch (start us, length us, event | category | flops | bytes accessed | tf_op | source)
XLA Modules:
  0.0 83.3 jit_solution(11610686314490499742)
XLA Ops:
  0.0 0.0 copy-start
  0.0 1.0 %copy-done = bf16[512,512]{1,0:T(8,128)(2,1)S(1)} copy-done((bf16[512,512]{1,0:T(8,128)(2,1)S(1)}, bf16[512,512]{1,0:T(8,128)(2,1)}, u32[]{:S(2)}) %copy-start) | copy-done | bytes 524312
  1.0 0.0 copy-start.1
  1.0 0.7 copy-done.1
  1.7 0.0 copy-start.2
  1.7 0.7 copy-done.2
  2.4 79.8 %gather_square.1 = (f32[512,512]{1,0:T(8,128)S(1)}, f32[1,512]{1,0:T(1,128)S(1)}) custom-call(bf16[512,512]{1,0:T(8,128)(2,1)S(1)} %copy-done, s32[2,2]{1,0:T(2,128)S(1)} %copy-done.1, s32[2,2]{1,0:T(2,128)S(1)} %copy-done.2), custom_call_target="tpu_custom_call" | custom-call | tf_op jit(solution)/shard_map/gather_square/pallas_call | solution.py:326
  82.2 1.1 %broadcast_multiply_fusion = f32[512,512]{1,0:T(8,128)} fusion(f32[512,512]{1,0:T(8,128)S(1)} %get-tuple-element.7, f32[512]{0:T(512)S(1)} %bitcast.1), kind=kLoop, calls=%fused_computation | loop fusion | flops 262144 | bytes 2099200 | tf_op jit(solution)/shard_map/mul | solution.py:362
  (1 shorter events, 0.0 us)
Async XLA Ops:
  0.0 1.0 %copy-start = (bf16[512,512]{1,0:T(8,128)(2,1)S(1)}, bf16[512,512]{1,0:T(8,128)(2,1)}, u32[]{:S(2)}) copy-start(bf16[512,512]{1,0:T(8,128)(2,1)} %m_ref.1) | copy-start | bytes 1572868
  1.0 0.7 copy-start.1
  1.7 0.7 copy-start.2

commit v2 on v1

v2 whole, which is shorter than its diff:
```python
import jax
import jax.numpy as jnp
from jax import lax
from jax.experimental import pallas as pl
from jax.experimental.pallas import tpu as pltpu
from jax.sharding import PartitionSpec as P

MESH = pl.DeviceIdType.MESH
T = 256
N = 2 * T
LANES = 128
SLOT = 2 * T
BODY = 3 * SLOT
ROWS = BODY + 16
CUT = 784
HALF = ((0, CUT), (CUT, ROWS - CUT))
XCUT = (HALF, ((0, 464), (464, 448), (912, 384), (1296, 256)))
PAIRS = tuple((t, s) for t in range(4) for s in range(3) if s <= t)


def kernel(
    m_hbm, masks_hbm, infl_ref, scale_ref,
    m_ref, masks, abuf, bbuf, ad, bd, acc, tot, part,
    ys, yr, zs, zr, xs, xr, fs, fr, cs, cr, ss, sr, ts, tr, osem, isem,
):
    row = lax.axis_index("row")
    col = lax.axis_index("col")
    y, z = row // 4, row % 4
    x, h, core = col // 4, (col // 2) % 2, col % 2
    hi = z // 2
    yup, ydn = (y + 1) % 4, (y + 3) % 4
    xup, xdn = (x + 1) % 4, (x + 3) % 4
    zorder = (z, 1 - z + 4 * hi, 2 - hi, 3 - 3 * hi)
    horder = (h, 1 - h)

    def col_of(xx, hh, kk):
        return xx * 4 + hh * 2 + kk

    loads = [
        pltpu.make_async_copy(src, dst, isem.at[n])
        for n, (src, dst) in enumerate(((masks_hbm, masks), (m_hbm, m_ref)))
    ]
    for load in loads:
        load.start()

    barrier = pltpu.get_barrier_semaphore()

    def greet(d, _):
        pl.semaphore_signal(barrier, inc=1, device_id=((row + d) % 16, col), device_id_type=MESH)
        return 0

    lax.fori_loop(1, 16, greet, 0)
    for c in (col_of(xup, h, core), col_of(xdn, h, core), col_of(x, 1 - h, core), col_of(x, h, 1 - core)):
        pl.semaphore_signal(barrier, inc=1, device_id=(row, c), device_id_type=MESH)

    for load in loads:
        load.wait()
    flags = [masks[0, 0], masks[0, 1], masks[1, 0], masks[1, 1]]
    ranks = [0, flags[0], flags[0] + flags[1], flags[0] + flags[1] + flags[2]]
    here = {(t, s): jnp.logical_and(flags[t] == 1, ranks[t] == s) for t, s in PAIRS}
    mine_b = row
    mine_a = col
    for s in range(3):
        for r in range(0, T, 64):
            value = jnp.zeros((64, T), jnp.bfloat16)
            for t in range(s, 4):
                i, j = t // 2, t % 2
                tile = m_ref[i * T + r : i * T + r + 64, j * T : (j + 1) * T]
                value = lax.select(here[t, s], tile, value)
            for e in range(2):
                at = pl.ds(s * SLOT + e * T + r, 64)
                bbuf[mine_b, at, :] = value[:, e * LANES : (e + 1) * LANES]
                abuf[mine_a, at, :] = value[:, e * LANES : (e + 1) * LANES]
    line = lax.broadcasted_iota(jnp.int32, (16, LANES), 0)
    weights = jnp.zeros((16, LANES), jnp.float32)
    for q, (t, s) in enumerate(PAIRS):
        weights = jnp.where(line == q, here[t, s].astype(jnp.float32), weights)
    weights = weights.astype(jnp.bfloat16)
    bbuf[mine_b, pl.ds(BODY, 16), :] = weights
    abuf[mine_a, pl.ds(BODY, 16), :] = weights

    pl.semaphore_wait(barrier, 19)

    def whole(buf, k, send, recv, device):
        return pltpu.make_async_remote_copy(
            src_ref=buf.at[k], dst_ref=buf.at[k], send_sem=send, recv_sem=recv,
            device_id=device, device_id_type=MESH,
        )

    def half(buf, k, p, send, recv, device):
        at = buf.at[k, pl.ds(*HALF[p]), :]
        return pltpu.make_async_remote_copy(
            src_ref=at, dst_ref=at, send_sem=send, recv_sem=recv,
            device_id=device, device_id_type=MESH,
        )

    def y_copy(i, way, piece):
        to = ((yup, ydn)[way] * 4 + z, col)
        if piece < 2:
            which, origin = (way, 1 - way)[piece], y
        else:
            which, origin = way, (ydn, yup)[way]
        return half(bbuf, origin * 4 + zorder[i], which, ys.at[i, way, piece], yr.at[i, way, piece], to)

    def y_arrival(i, way, piece):
        if piece < 2:
            which, origin = (way, 1 - way)[piece], (ydn, yup)[way]
        else:
            which, origin = way, (y + 2) % 4
        return half(bbuf, origin * 4 + zorder[i], which, ys.at[i, way, piece], yr.at[i, way, piece], ((yup, ydn)[way] * 4 + z, col))

    def x_piece(i, origin, q, send, recv, way):
        at = abuf.at[col_of(origin, horder[i], core), pl.ds(*XCUT[i][q]), :]
        return pltpu.make_async_remote_copy(
            src_ref=at, dst_ref=at, send_sem=send, recv_sem=recv,
            device_id=(row, col_of((xup, xdn)[way], h, core)), device_id_type=MESH,
        )

    def x_copy(i, way, q):
        return x_piece(i, x, q, xs.at[i, way, q], xr.at[i, way, q], way)

    def x_arrival(i, way, q):
        return x_piece(i, (xdn, xup)[way], q, xs.at[i, way, q], xr.at[i, way, q], way)

    def x_forward(i, q):
        return x_piece(i, (xdn, xup)[q % 2], q, fs.at[i, q], fr.at[i, q], q % 2)

    def x_forwarded(i, q):
        return x_piece(i, (x + 2) % 4, q, fs.at[i, q], fr.at[i, q], q % 2)

    def s_piece(i, d, q, kk):
        at = abuf.at[col_of((x + d) % 4, horder[i], kk), pl.ds(*XCUT[i][q]), :]
        return pltpu.make_async_remote_copy(
            src_ref=at, dst_ref=at, send_sem=ss.at[i, d, q], recv_sem=sr.at[i, d, q],
            device_id=(row, col_of(x, h, 1 - core)), device_id_type=MESH,
        )

    def s_copy(i, d, q):
        return s_piece(i, d, q, core)

    def s_arrival(i, d):
        for q in range(len(XCUT[i])):
            s_piece(i, d, q, 1 - core).wait_recv()

    def cross(q, k=None):
        at = abuf.at[mine_a if k is None else k, pl.ds(*XCUT[1][q]), :]
        return pltpu.make_async_remote_copy(
            src_ref=at, dst_ref=at, send_sem=cs.at[q], recv_sem=cr.at[q],
            device_id=(row, col_of(x, 1 - h, core)), device_id_type=MESH,
        )

    def crossed(q):
        return cross(q, col_of(x, 1 - h, core))

    z_up = whole(bbuf, row, zs.at[0], zr.at[z], (row + 1, col))
    z_down = whole(bbuf, row, zs.at[1], zr.at[z], (row - 1, col))
    has_up, has_down = z < 3, z > 0
    interior = jnp.logical_and(has_up, has_down)
    at_end = jnp.logical_not(interior)

    def z_forward(i):
        to = y * 4 + (3 - z if i == 1 else 3 * hi)
        k = y * 4 + zorder[i]
        return whole(bbuf, k, zs.at[1 + i], zr.at[zorder[i]], (to, col))

    def z_arrival(i):
        k = y * 4 + zorder[i]
        return whole(bbuf, k, zs.at[1 + i], zr.at[zorder[i]], (y * 4 + (z + 1) % 4, col))

    def y_send(i):
        for piece in range(2):
            for way in range(2):
                y_copy(i, way, piece).start()

    def y_turn(i):
        for way in range(2):
            y_arrival(i, way, 0).wait_recv()
            y_copy(i, way, 2).start()

    def x_send(i, q):
        for way in (q % 2, 1 - q % 2):
            x_copy(i, way, q).start()

    def x_cross(q):
        crossed(q).wait_recv()
        x_send(1, q)
        s_copy(1, 0, q).start()

    def x_turn(i, q):
        x_arrival(i, q % 2, q).wait_recv()
        x_forward(i, q).start()
        s_copy(i, (3, 1)[q % 2], q).start()

    def x_near(i, q):
        x_arrival(i, 1 - q % 2, q).wait_recv()
        s_copy(i, (1, 3)[q % 2], q).start()

    def x_far(i, q):
        x_forwarded(i, q).wait_recv()
        s_copy(i, 2, q).start()

    def z_turn(i):
        z_arrival(i).wait_recv()
        pl.when(interior)(lambda: z_forward(i).start())

    def s_rest(i):
        for d in range(4):
            s_arrival(i, d)

    def y_rest(i):
        for way in range(2):
            y_arrival(i, way, 1).wait_recv()
            y_arrival(i, way, 2).wait_recv()

    def expand(buf, k, to):
        ext = buf[k, pl.ds(BODY, 16), :].astype(jnp.float32)
        w = {
            at: jnp.broadcast_to(ext[q : q + 1, :], (16, LANES)).astype(jnp.bfloat16)[None]
            for q, at in enumerate(PAIRS)
        }
        for t in range(4):
            i, j = t // 2, t % 2
            for e in range(2):
                value = None
                for s in range(min(t, 2) + 1):
                    part_of = buf[k, pl.ds(s * SLOT + e * T, T), :]
                    term = part_of.reshape(16, 16, LANES) * w[t, s]
                    value = term if value is None else value + term
                left = j * T + e * LANES
                to[i * T : (i + 1) * T, left : left + LANES] = value.reshape(T, LANES)

    def product(k):
        expand(abuf, k, ad)
        expand(bbuf, k, bd)
        acc[...] += jnp.dot(ad[...], bd[...], preferred_element_type=jnp.float32)

    def products(i, first, count=4, stride=1):
        def one(n, _):
            product(((first + n * stride) % 4) * 4 + zorder[i])
            return 0

        lax.fori_loop(0, count, one, 0)

    near = hi == h
    far = hi != h

    def late(first, count):
        @pl.when(far)
        def _():
            products(0, x + first, count, 2)
            products(1, x + first, count, 2)

        pl.when(near)(lambda: products(2, x + first, count, 2))

    @pl.when(has_up)
    def _():
        z_up.start()

    @pl.when(has_down)
    def _():
        z_down.start()

    y_send(0)
    for q in range(2):
        x_send(0, q)
        s_copy(0, 0, q).start()
    cross(0).start()
    acc[...] = jnp.zeros_like(acc)
    y_turn(0)
    x_turn(0, 0)
    x_turn(0, 1)
    z_turn(1)
    pl.when(interior)(lambda: z_turn(2))
    y_send(1)
    cross(1).start()
    for q in range(2):
        x_near(0, q)
    for q in range(2):
        x_far(0, q)
    s_rest(0)
    y_rest(0)
    y_turn(1)
    pl.when(near)(lambda: products(0, y))
    pl.when(interior)(lambda: z_turn(3))
    pl.when(at_end)(lambda: z_arrival(2).wait_recv())
    y_send(2)
    cross(2).start()
    cross(3).start()
    x_cross(0)
    y_rest(1)
    pl.when(near)(lambda: products(1, y))
    x_turn(1, 0)
    x_near(1, 0)
    y_turn(2)
    pl.when(interior)(lambda: y_send(3))
    x_cross(1)
    x_far(1, 0)
    x_turn(1, 1)
    x_near(1, 1)

    @pl.when(at_end)
    def _():
        z_arrival(3).wait_recv()
        y_send(3)

    y_rest(2)

    @pl.when(far)
    def _():
        products(2, y)
        products(3, y, 1)

    x_cross(2)
    x_far(1, 1)
    y_turn(3)
    x_cross(3)
    x_turn(1, 2)
    x_turn(1, 3)
    x_near(1, 2)
    x_near(1, 3)
    s_arrival(1, 0)
    late(0, 1)
    x_far(1, 2)
    x_far(1, 3)
    s_arrival(1, 1)
    s_arrival(1, 3)
    late(1, 2)
    for way in range(2):
        y_arrival(3, way, 1).wait_recv()
    pl.when(jnp.logical_and(near, y != (x + 2) % 4))(lambda: products(3, y, 1))
    for d in (1, 3):
        pl.when(jnp.logical_or(far, (y + d) % 4 != (x + 2) % 4))(lambda d=d: products(3, y + d, 1))
    for way in range(2):
        y_arrival(3, way, 2).wait_recv()
    pl.when(jnp.logical_or(far, y != x))(lambda: products(3, y + 2, 1))
    s_arrival(1, 2)

    @pl.when(far)
    def _():
        products(0, x + 2, 1)
        products(1, x + 2, 1)

    @pl.when(near)
    def _():
        products(2, x + 2, 1)
        products(3, x + 2, 1)

    sums = jnp.zeros((8, N), jnp.float32)
    pieces = [[None, None], [None, None]]
    for i in range(2):
        keep = [(masks[2 + i, j] == 1).astype(jnp.float32) for j in range(2)]
        for r in range(i * T, (i + 1) * T, 32):
            for j in range(2):
                at = (slice(r, r + 32), slice(j * T, (j + 1) * T))
                p = acc[at]
                v = p * p * keep[j]
                acc[at] = v
                v = v.reshape(4, 8, T).sum(axis=0)
                pieces[i][j] = v if pieces[i][j] is None else pieces[i][j] + v
    sums = jnp.concatenate([pieces[0][j] + pieces[1][j] for j in range(2)], axis=1)
    sums = jnp.sum(sums, axis=0, keepdims=True)
    part[...] = sums
    tot[row] = sums

    def t_copy(d, i):
        to = (y + d) % 4 * 4 + zorder[i]
        return pltpu.make_async_remote_copy(
            src_ref=part, dst_ref=tot.at[row], send_sem=ts.at[d, i], recv_sem=tr.at[row],
            device_id=(to, col), device_id_type=MESH,
        )

    def t_arrival(d):
        k = (row + d) % 16
        return pltpu.make_async_remote_copy(
            src_ref=part, dst_ref=tot.at[k], send_sem=ts.at[0, 0], recv_sem=tr.at[k],
            device_id=(k, col), device_id_type=MESH,
        )

    peers = [(d, i) for d in (2, 1, 3, 0) for i in (3, 2, 1, 0) if d or i]
    peers.sort(key=lambda at: -(min(at[0], 2) % 3 - (at[0] == 3) + at[1]))
    for d, i in peers:
        t_copy(d, i).start()
    out = pltpu.make_async_copy(acc, infl_ref, osem)
    out.start()
    lax.fori_loop(1, 16, lambda d, _: (t_arrival(d).wait_recv(), 0)[1], 0)
    total = tot[0]
    for d in range(1, 16):
        total = total + tot[d]
    scale_ref[...] = 1.0 / total
    out.wait()

    for d, i in peers:
        t_copy(d, i).wait_send()
    for i in range(4):
        for way in range(2):
            for piece in range(3):
                y_copy(i, way, piece).wait_send()
    for i in range(2):
        for q in range(len(XCUT[i])):
            for way in range(2):
                x_copy(i, way, q).wait_send()
            x_forward(i, q).wait_send()
            for d in range(4):
                s_copy(i, d, q).wait_send()
    for q in range(4):
        cross(q).wait_send()

    @pl.when(has_up)
    def _():
        z_up.wait_send()

    @pl.when(has_down)
    def _():
        z_down.wait_send()

    @pl.when(interior)
    def _():
        for i in range(1, 4):
            z_forward(i).wait_send()


def solution(mesh):
    def step(matrix, in_mask, out_mask):
        total_rows = float(N * mesh.shape["row"])
        dma = pltpu.SemaphoreType.DMA
        inflated, scale = pl.pallas_call(
            kernel,
            out_shape=(
                jax.ShapeDtypeStruct((N, N), jnp.float32),
                jax.ShapeDtypeStruct((1, N), jnp.float32),
            ),
            in_specs=[
                pl.BlockSpec(memory_space=pltpu.HBM),
                pl.BlockSpec(memory_space=pltpu.HBM),
            ],
            out_specs=(
                pl.BlockSpec(memory_space=pl.ANY),
                pl.BlockSpec(memory_space=pltpu.VMEM),
            ),
            scratch_shapes=[
                pltpu.VMEM((N, N), jnp.bfloat16),
                pltpu.SMEM((4, 2), jnp.int32),
                pltpu.VMEM((16, ROWS, LANES), jnp.bfloat16),
                pltpu.VMEM((16, ROWS, LANES), jnp.bfloat16),
                pltpu.VMEM((N, N), jnp.bfloat16),
                pltpu.VMEM((N, N), jnp.bfloat16),
                pltpu.VMEM((N, N), jnp.float32),
                pltpu.VMEM((16, 1, N), jnp.float32),
                pltpu.VMEM((1, N), jnp.float32),
                dma((4, 2, 3)), dma((4, 2, 3)),
                dma((5,)), dma((4,)),
                dma((2, 2, 4)), dma((2, 2, 4)),
                dma((2, 4)), dma((2, 4)),
                dma((4,)), dma((4,)),
                dma((2, 4, 4)), dma((2, 4, 4)),
                dma((4, 4)), dma((16,)),
                dma, dma((3,)),
            ],
            compiler_params=pltpu.CompilerParams(
                collective_id=0, has_side_effects=True, vmem_limit_bytes=40 * 1024 * 1024
            ),
            name="gather_square",
        )(matrix, jnp.concatenate([in_mask, out_mask]))
        return (total_rows * inflated) * scale

    placed = (P("row", "col"), P("row", "col"), P("row", "col"))
    return jax.shard_map(
        step, mesh=mesh, in_specs=placed, out_specs=P("row", "col"), check_vma=False
    )
```

time: 83.5 us -> 79.7 us (0.954)
  the two profiles are of different devices: /device:TPU:1 before, /device:TPU:2 now
where the time goes in v2:
time: 79.7 us; the launch traced here: 79.6 us
  Pallas kernels  76.8 us (96%)
  other arithmetic  1.8 us (2%)
  local copies, waits for them, and re-layouts  1.04 us (1%)
    pallas_call x1, Pallas kernels, step(): pl.pallas_call(kernel, out_shape=(jax.ShapeDtypeStruct((N, N), jnp.float3...  76.8 us

profile of v2, /device:TPU:2, one launch (start us, length us, event | category | flops | bytes accessed | tf_op | source)
XLA Modules:
  0.0 79.6 jit_solution(1837397218927136332)
XLA Ops:
  0.0 0.7 pad_add_fusion.masks_hbm
  0.7 0.0 copy-start
  0.7 1.0 %copy-done = bf16[512,512]{1,0:T(8,128)(2,1)S(1)} copy-done((bf16[512,512]{1,0:T(8,128)(2,1)S(1)}, bf16[512,512]{1,0:T(8,128)(2,1)}, u32[]{:S(2)}) %copy-start) | copy-done | bytes 524312
  1.7 76.8 %gather_square.1 = (f32[512,512]{1,0:T(8,128)S(1)}, f32[1,512]{1,0:T(1,128)S(1)}) custom-call(bf16[512,512]{1,0:T(8,128)(2,1)S(1)} %copy-done, s32[4,2]{1,0:T(4,128)S(1)} %pad_add_fusion.masks_hbm), custom_call_target="tpu_custom_call" | custom-call | tf_op jit(solution)/shard_map/gather_square/pallas_call | solution.py:426
  78.5 1.1 %broadcast_multiply_fusion = f32[512,512]{1,0:T(8,128)} fusion(f32[512,512]{1,0:T(8,128)S(1)} %get-tuple-element.7, f32[512]{0:T(512)S(1)} %bitcast.1), kind=kLoop, calls=%fused_computation | loop fusion | flops 262144 | bytes 2099200 | tf_op jit(solution)/shard_map/mul | solution.py:464
  (1 shorter events, 0.0 us)
Async XLA Ops:
  0.7 1.0 %copy-start = (bf16[512,512]{1,0:T(8,128)(2,1)S(1)}, bf16[512,512]{1,0:T(8,128)(2,1)}, u32[]{:S(2)}) copy-start(bf16[512,512]{1,0:T(8,128)(2,1)} %m_hbm.1) | copy-start | bytes 1572868

commit v3 on v2

--- a/solution.py
+++ b/solution.py
@@ -212,7 +212,7 @@
             y_arrival(i, way, 1).wait_recv()
             y_arrival(i, way, 2).wait_recv()
 
-    def expand(buf, k, to):
+    def expand(buf, k, to, r0, c0):
         ext = buf[k, pl.ds(BODY, 16), :].astype(jnp.float32)
         w = {
             at: jnp.broadcast_to(ext[q : q + 1, :], (16, LANES)).astype(jnp.bfloat16)[None]
@@ -227,16 +227,38 @@
                     term = part_of.reshape(16, 16, LANES) * w[t, s]
                     value = term if value is None else value + term
                 left = j * T + e * LANES
-                to[i * T : (i + 1) * T, left : left + LANES] = value.reshape(T, LANES)
-
-    def product(k):
-        expand(abuf, k, ad)
-        expand(bbuf, k, bd)
-        acc[...] += jnp.dot(ad[...], bd[...], preferred_element_type=jnp.float32)
+                to[pl.ds(r0 + i * T, T), pl.ds(c0 + left, LANES)] = value.reshape(T, LANES)
+
+    def open_a(i, first, count=4, stride=1):
+        def one(n, _):
+            k = (first + n // 2 * stride) % 4 * 4 + 2 * horder[i] + n % 2
+            expand(abuf, k, ad, 0, pl.multiple_of(k * N, N))
+            return 0
+
+        lax.fori_loop(0, 2 * count, one, 0)
+
+    def open_b(i, first, count=4, stride=1):
+        def one(n, _):
+            k = (first + n * stride) % 4 * 4 + zorder[i]
+            expand(bbuf, k, bd, pl.multiple_of(k * N, N), 0)
+            return 0
+
+        lax.fori_loop(0, count, one, 0)
+
+    def multiply(k, blocks):
+        at = pl.ds(pl.multiple_of(k * N, N), blocks * N)
+        acc[...] += jnp.dot(ad[:, at], bd[at, :], preferred_element_type=jnp.float32)
 
     def products(i, first, count=4, stride=1):
         def one(n, _):
-            product(((first + n * stride) % 4) * 4 + zorder[i])
+            multiply((first + n * stride) % 4 * 4 + zorder[i], 1)
+            return 0
+
+        lax.fori_loop(0, count, one, 0)
+
+    def doubles(hh, first, count=4, stride=1):
+        def one(n, _):
+            multiply((first + n * stride) % 4 * 4 + 2 * hh, 2)
             return 0
 
         lax.fori_loop(0, count, one, 0)
@@ -245,11 +267,8 @@
     far = hi != h
 
     def late(first, count):
-        @pl.when(far)
-        def _():
-            products(0, x + first, count, 2)
-            products(1, x + first, count, 2)
-
+        open_a(1, x + first, count, 2)
+        pl.when(far)(lambda: doubles(hi, x + first, count, 2))
         pl.when(near)(lambda: products(2, x + first, count, 2))
 
     @pl.when(has_up)
@@ -272,7 +291,6 @@
     z_turn(1)
     pl.when(interior)(lambda: z_turn(2))
     y_send(1)
-    cross(1).start()
     for q in range(2):
         x_near(0, q)
     for q in range(2):
@@ -280,7 +298,9 @@
     s_rest(0)
     y_rest(0)
     y_turn(1)
-    pl.when(near)(lambda: products(0, y))
+    cross(1).start()
+    open_a(0, x)
+    open_b(0, y)
     pl.when(interior)(lambda: z_turn(3))
     pl.when(at_end)(lambda: z_arrival(2).wait_recv())
     y_send(2)
@@ -288,7 +308,8 @@
     cross(3).start()
     x_cross(0)
     y_rest(1)
-    pl.when(near)(lambda: products(1, y))
+    open_b(1, y)
+    pl.when(near)(lambda: doubles(h, y))
     x_turn(1, 0)
     x_near(1, 0)
     y_turn(2)
@@ -304,6 +325,9 @@
         y_send(3)
 
     y_rest(2)
+
+    open_b(2, y)
+    open_b(3, y, 1)
 
     @pl.when(far)
     def _():
@@ -322,28 +346,22 @@
     late(0, 1)
     x_far(1, 2)
     x_far(1, 3)
+    for way in range(2):
+        y_arrival(3, way, 1).wait_recv()
+    open_b(3, y + 1, 2, 2)
+    pl.when(far)(lambda: products(3, y + 1, 2, 2))
     s_arrival(1, 1)
     s_arrival(1, 3)
     late(1, 2)
-    for way in range(2):
-        y_arrival(3, way, 1).wait_recv()
-    pl.when(jnp.logical_and(near, y != (x + 2) % 4))(lambda: products(3, y, 1))
-    for d in (1, 3):
-        pl.when(jnp.logical_or(far, (y + d) % 4 != (x + 2) % 4))(lambda d=d: products(3, y + d, 1))
+    for d in (0, 1, 3):
+        pl.when(jnp.logical_and(near, (y + d) % 4 != (x + 2) % 4))(lambda d=d: products(3, y + d, 1))
     for way in range(2):
         y_arrival(3, way, 2).wait_recv()
+    open_b(3, y + 2, 1)
     pl.when(jnp.logical_or(far, y != x))(lambda: products(3, y + 2, 1))
     s_arrival(1, 2)
-
-    @pl.when(far)
-    def _():
-        products(0, x + 2, 1)
-        products(1, x + 2, 1)
-
-    @pl.when(near)
-    def _():
-        products(2, x + 2, 1)
-        products(3, x + 2, 1)
+    open_a(1, x + 2, 1)
+    doubles(1 - h, x + 2, 1)
 
     sums = jnp.zeros((8, N), jnp.float32)
     pieces = [[None, None], [None, None]]
@@ -442,8 +460,8 @@
                 pltpu.SMEM((4, 2), jnp.int32),
                 pltpu.VMEM((16, ROWS, LANES), jnp.bfloat16),
                 pltpu.VMEM((16, ROWS, LANES), jnp.bfloat16),
-                pltpu.VMEM((N, N), jnp.bfloat16),
-                pltpu.VMEM((N, N), jnp.bfloat16),
+                pltpu.VMEM((N, 16 * N), jnp.bfloat16),
+                pltpu.VMEM((16 * N, N), jnp.bfloat16),
                 pltpu.VMEM((N, N), jnp.float32),
                 pltpu.VMEM((16, 1, N), jnp.float32),
                 pltpu.VMEM((1, N), jnp.float32),

time: 79.7 us -> 79 us (level)
  Pallas kernels: 76.8 us -> 76 us
where the time goes in v3:
time: 79 us; the launch traced here: 78.9 us
  Pallas kernels  76 us (96%)
  other arithmetic  1.8 us (2%)
  local copies, waits for them, and re-layouts  1.04 us (1%)
    pallas_call x1, Pallas kernels, step(): pl.pallas_call(kernel, out_shape=(jax.ShapeDtypeStruct((N, N), jnp.float3...  76 us

profile of v3, /device:TPU:2, one launch (start us, length us, event | category | flops | bytes accessed | tf_op | source)
XLA Modules:
  0.0 78.9 jit_solution(2466886477114743535)
XLA Ops:
  0.0 0.7 pad_add_fusion.masks_hbm
  0.7 0.0 copy-start
  0.7 1.0 %copy-done = bf16[512,512]{1,0:T(8,128)(2,1)S(1)} copy-done((bf16[512,512]{1,0:T(8,128)(2,1)S(1)}, bf16[512,512]{1,0:T(8,128)(2,1)}, u32[]{:S(2)}) %copy-start) | copy-done | bytes 524312
  1.7 76.0 %gather_square.1 = (f32[512,512]{1,0:T(8,128)S(1)}, f32[1,512]{1,0:T(1,128)S(1)}) custom-call(bf16[512,512]{1,0:T(8,128)(2,1)S(1)} %copy-done, s32[4,2]{1,0:T(4,128)S(1)} %pad_add_fusion.masks_hbm), custom_call_target="tpu_custom_call" | custom-call | tf_op jit(solution)/shard_map/gather_square/pallas_call | solution.py:444
  77.8 1.1 %broadcast_multiply_fusion = f32[512,512]{1,0:T(8,128)} fusion(f32[512,512]{1,0:T(8,128)S(1)} %get-tuple-element.7, f32[512]{0:T(512)S(1)} %bitcast.1), kind=kLoop, calls=%fused_computation | loop fusion | flops 262144 | bytes 2099200 | tf_op jit(solution)/shard_map/mul | solution.py:482
  (1 shorter events, 0.0 us)
Async XLA Ops:
  0.7 1.0 %copy-start = (bf16[512,512]{1,0:T(8,128)(2,1)S(1)}, bf16[512,512]{1,0:T(8,128)(2,1)}, u32[]{:S(2)}) copy-start(bf16[512,512]{1,0:T(8,128)(2,1)} %m_hbm.1) | copy-start | bytes 1572868

commit v4 on v3

--- a/solution.py
+++ b/solution.py
@@ -383,16 +383,14 @@
     def t_copy(d, i):
         to = (y + d) % 4 * 4 + zorder[i]
         return pltpu.make_async_remote_copy(
-            src_ref=part, dst_ref=tot.at[row], send_sem=ts.at[d, i], recv_sem=tr.at[row],
+            src_ref=part, dst_ref=tot.at[row], send_sem=ts, recv_sem=tr,
             device_id=(to, col), device_id_type=MESH,
         )
 
-    def t_arrival(d):
-        k = (row + d) % 16
-        return pltpu.make_async_remote_copy(
-            src_ref=part, dst_ref=tot.at[k], send_sem=ts.at[0, 0], recv_sem=tr.at[k],
-            device_id=(k, col), device_id_type=MESH,
-        )
+    t_all = pltpu.make_async_remote_copy(
+        src_ref=tot.at[pl.ds(0, 15)], dst_ref=tot.at[pl.ds(0, 15)], send_sem=ts, recv_sem=tr,
+        device_id=((row + 1) % 16, col), device_id_type=MESH,
+    )
 
     peers = [(d, i) for d in (2, 1, 3, 0) for i in (3, 2, 1, 0) if d or i]
     peers.sort(key=lambda at: -(min(at[0], 2) % 3 - (at[0] == 3) + at[1]))
@@ -400,15 +398,7 @@
         t_copy(d, i).start()
     out = pltpu.make_async_copy(acc, infl_ref, osem)
     out.start()
-    lax.fori_loop(1, 16, lambda d, _: (t_arrival(d).wait_recv(), 0)[1], 0)
-    total = tot[0]
-    for d in range(1, 16):
-        total = total + tot[d]
-    scale_ref[...] = 1.0 / total
-    out.wait()
-
-    for d, i in peers:
-        t_copy(d, i).wait_send()
+
     for i in range(4):
         for way in range(2):
             for piece in range(3):
@@ -435,6 +425,15 @@
     def _():
         for i in range(1, 4):
             z_forward(i).wait_send()
+
+    t_all.wait_recv()
+    total = tot[0]
+    for d in range(1, 16):
+        total = total + tot[d]
+    scale_ref[...] = 1.0 / total
+    out.wait()
+
+    t_all.wait_send()
 
 
 def solution(mesh):
@@ -471,7 +470,7 @@
                 dma((2, 4)), dma((2, 4)),
                 dma((4,)), dma((4,)),
                 dma((2, 4, 4)), dma((2, 4, 4)),
-                dma((4, 4)), dma((16,)),
+                dma, dma,
                 dma, dma((3,)),
             ],
             compiler_params=pltpu.CompilerParams(

time: 79 us -> 78.6 us (level)
  no operation moved by 1% of the time
where the time goes in v4:
time: 78.6 us; the launch traced here: 78.5 us
  Pallas kernels  75.6 us (96%)
  other arithmetic  1.8 us (2%)
  local copies, waits for them, and re-layouts  1.04 us (1%)
    pallas_call x1, Pallas kernels, step(): pl.pallas_call(kernel, out_shape=(jax.ShapeDtypeStruct((N, N), jnp.float3...  75.6 us

profile of v4, /device:TPU:2, one launch (start us, length us, event | category | flops | bytes accessed | tf_op | source)
XLA Modules:
  0.0 78.5 jit_solution(2454815173816373420)
XLA Ops:
  0.0 0.7 pad_add_fusion.masks_hbm
  0.7 0.0 copy-start
  0.7 1.0 %copy-done = bf16[512,512]{1,0:T(8,128)(2,1)S(1)} copy-done((bf16[512,512]{1,0:T(8,128)(2,1)S(1)}, bf16[512,512]{1,0:T(8,128)(2,1)}, u32[]{:S(2)}) %copy-start) | copy-done | bytes 524312
  1.7 75.6 %gather_square.1 = (f32[512,512]{1,0:T(8,128)S(1)}, f32[1,512]{1,0:T(1,128)S(1)}) custom-call(bf16[512,512]{1,0:T(8,128)(2,1)S(1)} %copy-done, s32[4,2]{1,0:T(4,128)S(1)} %pad_add_fusion.masks_hbm), custom_call_target="tpu_custom_call" | custom-call | tf_op jit(solution)/shard_map/gather_square/pallas_call | solution.py:443
  77.4 1.1 %broadcast_multiply_fusion = f32[512,512]{1,0:T(8,128)} fusion(f32[512,512]{1,0:T(8,128)S(1)} %get-tuple-element.7, f32[512]{0:T(512)S(1)} %bitcast.1), kind=kLoop, calls=%fused_computation | loop fusion | flops 262144 | bytes 2099200 | tf_op jit(solution)/shard_map/mul | solution.py:481
  (1 shorter events, 0.0 us)
Async XLA Ops:
  0.7 1.0 %copy-start = (bf16[512,512]{1,0:T(8,128)(2,1)S(1)}, bf16[512,512]{1,0:T(8,128)(2,1)}, u32[]{:S(2)}) copy-start(bf16[512,512]{1,0:T(8,128)(2,1)} %m_hbm.1) | copy-start | bytes 1572868

commit v5 on v4

--- a/solution.py
+++ b/solution.py
@@ -14,7 +14,7 @@
 ROWS = BODY + 16
 CUT = 784
 HALF = ((0, CUT), (CUT, ROWS - CUT))
-XCUT = (HALF, ((0, 464), (464, 448), (912, 384), (1296, 256)))
+XCUT = (HALF, ((0, 480), (480, 448), (928, 384), (1312, 240)))
 PAIRS = tuple((t, s) for t in range(4) for s in range(3) if s <= t)
 
 
@@ -44,14 +44,19 @@
         load.start()
 
     barrier = pltpu.get_barrier_semaphore()
-
-    def greet(d, _):
-        pl.semaphore_signal(barrier, inc=1, device_id=((row + d) % 16, col), device_id_type=MESH)
-        return 0
-
-    lax.fori_loop(1, 16, greet, 0)
-    for c in (col_of(xup, h, core), col_of(xdn, h, core), col_of(x, 1 - h, core), col_of(x, h, 1 - core)):
-        pl.semaphore_signal(barrier, inc=1, device_id=(row, c), device_id_type=MESH)
+    has_up, has_down = z < 3, z > 0
+
+    def greet(r, c):
+        pl.semaphore_signal(barrier, inc=1, device_id=(r, c), device_id_type=MESH)
+
+    greet(row, col_of(x, 1 - h, core))
+    greet(yup * 4 + z, col)
+    greet(ydn * 4 + z, col)
+    pl.when(has_up)(lambda: greet(row + 1, col))
+    pl.when(has_down)(lambda: greet(row - 1, col))
+    greet(row, col_of(xup, h, core))
+    greet(row, col_of(xdn, h, core))
+    greet(row, col_of(x, h, 1 - core))
 
     for load in loads:
         load.wait()
@@ -79,7 +84,7 @@
     bbuf[mine_b, pl.ds(BODY, 16), :] = weights
     abuf[mine_a, pl.ds(BODY, 16), :] = weights
 
-    pl.semaphore_wait(barrier, 19)
+    pl.semaphore_wait(barrier, 6 + has_up.astype(jnp.int32) + has_down.astype(jnp.int32))
 
     def whole(buf, k, send, recv, device):
         return pltpu.make_async_remote_copy(
@@ -154,7 +159,6 @@
 
     z_up = whole(bbuf, row, zs.at[0], zr.at[z], (row + 1, col))
     z_down = whole(bbuf, row, zs.at[1], zr.at[z], (row - 1, col))
-    has_up, has_down = z < 3, z > 0
     interior = jnp.logical_and(has_up, has_down)
     at_end = jnp.logical_not(interior)
 
@@ -305,7 +309,6 @@
     pl.when(at_end)(lambda: z_arrival(2).wait_recv())
     y_send(2)
     cross(2).start()
-    cross(3).start()
     x_cross(0)
     y_rest(1)
     open_b(1, y)
@@ -313,6 +316,7 @@
     x_turn(1, 0)
     x_near(1, 0)
     y_turn(2)
+    cross(3).start()
     pl.when(interior)(lambda: y_send(3))
     x_cross(1)
     x_far(1, 0)

time: 78.6 us -> 78.3 us (level)
  no operation moved by 1% of the time
where the time goes in v5:
time: 78.3 us; the launch traced here: 78.2 us
  Pallas kernels  75.3 us (96%)
  other arithmetic  1.8 us (2%)
  local copies, waits for them, and re-layouts  1.04 us (1%)
    pallas_call x1, Pallas kernels, step(): pl.pallas_call(kernel, out_shape=(jax.ShapeDtypeStruct((N, N), jnp.float3...  75.3 us

profile of v5, /device:TPU:2, one launch (start us, length us, event | category | flops | bytes accessed | tf_op | source)
XLA Modules:
  0.0 78.2 jit_solution(8683086831883758768)
XLA Ops:
  0.0 0.7 pad_add_fusion.masks_hbm
  0.7 0.0 copy-start
  0.7 1.0 %copy-done = bf16[512,512]{1,0:T(8,128)(2,1)S(1)} copy-done((bf16[512,512]{1,0:T(8,128)(2,1)S(1)}, bf16[512,512]{1,0:T(8,128)(2,1)}, u32[]{:S(2)}) %copy-start) | copy-done | bytes 524312
  1.7 75.3 %gather_square.1 = (f32[512,512]{1,0:T(8,128)S(1)}, f32[1,512]{1,0:T(1,128)S(1)}) custom-call(bf16[512,512]{1,0:T(8,128)(2,1)S(1)} %copy-done, s32[4,2]{1,0:T(4,128)S(1)} %pad_add_fusion.masks_hbm), custom_call_target="tpu_custom_call" | custom-call | tf_op jit(solution)/shard_map/gather_square/pallas_call | solution.py:447
  77.1 1.1 %broadcast_multiply_fusion = f32[512,512]{1,0:T(8,128)} fusion(f32[512,512]{1,0:T(8,128)S(1)} %get-tuple-element.7, f32[512]{0:T(512)S(1)} %bitcast.1), kind=kLoop, calls=%fused_computation | loop fusion | flops 262144 | bytes 2099200 | tf_op jit(solution)/shard_map/mul | solution.py:485
  (1 shorter events, 0.0 us)
Async XLA Ops:
  0.7 1.0 %copy-start = (bf16[512,512]{1,0:T(8,128)(2,1)S(1)}, bf16[512,512]{1,0:T(8,128)(2,1)}, u32[]{:S(2)}) copy-start(bf16[512,512]{1,0:T(8,128)(2,1)} %m_hbm.1) | copy-start | bytes 1572868

commit v6 on v5

--- a/solution.py
+++ b/solution.py
@@ -19,9 +19,9 @@
 
 
 def kernel(
-    m_hbm, masks_hbm, infl_ref, scale_ref,
-    m_ref, masks, abuf, bbuf, ad, bd, acc, tot, part,
-    ys, yr, zs, zr, xs, xr, fs, fr, cs, cr, ss, sr, ts, tr, osem, isem,
+    m_hbm, masks_hbm, acc, scale_ref,
+    m_ref, masks, abuf, bbuf, ad, bd, tot, part,
+    ys, yr, zs, zr, xs, xr, fs, fr, cs, cr, ss, sr, ts, tr, isem,
 ):
     row = lax.axis_index("row")
     col = lax.axis_index("col")
@@ -400,8 +400,6 @@
     peers.sort(key=lambda at: -(min(at[0], 2) % 3 - (at[0] == 3) + at[1]))
     for d, i in peers:
         t_copy(d, i).start()
-    out = pltpu.make_async_copy(acc, infl_ref, osem)
-    out.start()
 
     for i in range(4):
         for way in range(2):
@@ -431,11 +429,8 @@
             z_forward(i).wait_send()
 
     t_all.wait_recv()
-    total = tot[0]
-    for d in range(1, 16):
-        total = total + tot[d]
+    total = jnp.sum(tot[...], axis=0)
     scale_ref[...] = 1.0 / total
-    out.wait()
 
     t_all.wait_send()
 
@@ -455,7 +450,7 @@
                 pl.BlockSpec(memory_space=pltpu.HBM),
             ],
             out_specs=(
-                pl.BlockSpec(memory_space=pl.ANY),
+                pl.BlockSpec(memory_space=pltpu.VMEM),
                 pl.BlockSpec(memory_space=pltpu.VMEM),
             ),
             scratch_shapes=[
@@ -465,7 +460,6 @@
                 pltpu.VMEM((16, ROWS, LANES), jnp.bfloat16),
                 pltpu.VMEM((N, 16 * N), jnp.bfloat16),
                 pltpu.VMEM((16 * N, N), jnp.bfloat16),
-                pltpu.VMEM((N, N), jnp.float32),
                 pltpu.VMEM((16, 1, N), jnp.float32),
                 pltpu.VMEM((1, N), jnp.float32),
                 dma((4, 2, 3)), dma((4, 2, 3)),
@@ -475,7 +469,7 @@
                 dma((4,)), dma((4,)),
                 dma((2, 4, 4)), dma((2, 4, 4)),
                 dma, dma,
-                dma, dma((3,)),
+                dma((3,)),
             ],
             compiler_params=pltpu.CompilerParams(
                 collective_id=0, has_side_effects=True, vmem_limit_bytes=40 * 1024 * 1024

time: 78.3 us -> 78.3 us (level)
  no operation moved by 1% of the time
where the time goes in v6:
time: 78.3 us; the launch traced here: 78.2 us
  Pallas kernels  75.3 us (96%)
  other arithmetic  1.8 us (2%)
  local copies, waits for them, and re-layouts  1.04 us (1%)
    pallas_call x1, Pallas kernels, step(): pl.pallas_call(kernel, out_shape=(jax.ShapeDtypeStruct((N, N), jnp.float3...  75.3 us

profile of v6, /device:TPU:2, one launch (start us, length us, event | category | flops | bytes accessed | tf_op | source)
XLA Modules:
  0.0 78.2 jit_solution(7349384859827866779)
XLA Ops:
  0.0 0.7 pad_add_fusion.masks_hbm
  0.7 0.0 copy-start
  0.7 1.0 %copy-done = bf16[512,512]{1,0:T(8,128)(2,1)S(1)} copy-done((bf16[512,512]{1,0:T(8,128)(2,1)S(1)}, bf16[512,512]{1,0:T(8,128)(2,1)}, u32[]{:S(2)}) %copy-start) | copy-done | bytes 524312
  1.7 75.3 %gather_square.1 = (f32[512,512]{1,0:T(8,128)S(1)}, f32[1,512]{1,0:T(1,128)S(1)}) custom-call(bf16[512,512]{1,0:T(8,128)(2,1)S(1)} %copy-done, s32[4,2]{1,0:T(4,128)S(1)} %pad_add_fusion.masks_hbm), custom_call_target="tpu_custom_call" | custom-call | tf_op jit(solution)/shard_map/gather_square/pallas_call | solution.py:442
  77.1 1.1 %broadcast_multiply_fusion = f32[512,512]{1,0:T(8,128)} fusion(f32[512,512]{1,0:T(8,128)S(1)} %get-tuple-element.7, f32[512]{0:T(512)S(1)} %bitcast.1), kind=kLoop, calls=%fused_computation | loop fusion | flops 262144 | bytes 2099200 | tf_op jit(solution)/shard_map/mul | solution.py:479
  (1 shorter events, 0.0 us)
Async XLA Ops:
  0.7 1.0 %copy-start = (bf16[512,512]{1,0:T(8,128)(2,1)S(1)}, bf16[512,512]{1,0:T(8,128)(2,1)}, u32[]{:S(2)}) copy-start(bf16[512,512]{1,0:T(8,128)(2,1)} %m_hbm.1) | copy-start | bytes 1572868
